TPU v7x, 128 devices: a whole 4x4x4 slice. The times are simulated.
128 devices in a mesh: img: 8 (over z, core), txt: 16 (over x, y).
Axes of the slice: x: 4, y: 4, z: 4, core: 2. Of those that a mesh axis runs over, the one named last changes fastest.
Arguments:
- teacher_image: bfloat16 [16384, 1280], P(('img', 'txt')), may hold values from -24 to 24
- teacher_text: bfloat16 [16384, 1280], P(('txt', 'img')), may hold values from -24 to 24
- student_image: bfloat16 [16384, 512], P(('img', 'txt')), may hold values from -24 to 24
- student_text: bfloat16 [16384, 512], P(('txt', 'img')), may hold values from -24 to 24
Outputs:
- loss: float32 [], replicated
- image_grad: float32 [16384, 512], P(('img', 'txt'))
- text_grad: float32 [16384, 512], P(('txt', 'img'))
All inputs are finite; a program needn't handle non-finite values.
Results may differ from a plain program's by a relative error of at most 0.0012.
Values may be sent and summed in bfloat16 or wider, within the bound.
A program may use at most 128 MiB of HBM per device.

v0:
```python
import math

import jax
import jax.numpy as jnp
from jax import lax
from jax.sharding import PartitionSpec as P


def pair_logits(
    image_teacher, image_student, text_teacher, text_student, scale_teacher, scale_student
):
    teacher_logit = (
        jnp.einsum("rd,cd->rc", image_teacher, text_teacher, preferred_element_type=jnp.float32)
        * scale_teacher
    )
    student_logit = (
        jnp.einsum("rd,cd->rc", image_student, text_student, preferred_element_type=jnp.float32)
        * scale_student
    )
    return (teacher_logit, student_logit)


def fold_columns(column_peak, column_total, logit):
    new_peak = jnp.maximum(column_peak, jnp.max(logit, axis=0))
    new_total = column_total * jnp.exp(column_peak - new_peak) + jnp.sum(
        jnp.exp(logit - new_peak[None, :]), axis=0
    )
    return (new_peak, new_total)


def split_delta(delta):
    delta_high = delta.astype(jnp.bfloat16)
    widened = lax.optimization_barrier(delta_high).astype(jnp.float32)
    delta_low = (delta - widened).astype(jnp.bfloat16)
    return (delta_high, delta_low)


def row_blocks(piece_rows):
    step_rows = math.gcd(piece_rows, 512)
    return [(offset, step_rows) for offset in range(0, piece_rows, step_rows)]


def local(teacher_image, teacher_text, student_image, student_text):
    scale_teacher = teacher_image.shape[1] ** (-0.5)
    scale_student = student_image.shape[1] ** (-0.5)
    text_teacher, text_student = (
        lax.all_gather(teacher_text, "img", axis=0, tiled=True),
        lax.all_gather(student_text, "img", axis=0, tiled=True),
    )
    tile_rows = teacher_image.shape[0] * lax.axis_size("txt")
    tile_cols = text_teacher.shape[0]
    row_empty = jnp.zeros((tile_rows,), jnp.float32)
    column_peak_empty = jnp.full((tile_cols,), -jnp.inf, jnp.float32)
    column_total_empty = jnp.zeros((tile_cols,), jnp.float32)
    image_teacher, image_student = (
        lax.all_gather(teacher_image, "txt", axis=0, tiled=True),
        lax.all_gather(student_image, "txt", axis=0, tiled=True),
    )
    pieces = (image_teacher, image_student)
    teacher_row_peak = row_empty
    teacher_row_total = row_empty
    student_row_peak = row_empty
    student_row_total = row_empty
    teacher_column_peak = column_peak_empty
    teacher_column_total = column_total_empty
    student_column_peak = column_peak_empty
    student_column_total = column_total_empty
    for offset, count in row_blocks(pieces[0].shape[0]):
        teacher_logit, student_logit = pair_logits(
            pieces[0][offset : offset + count],
            pieces[1][offset : offset + count],
            text_teacher,
            text_student,
            scale_teacher,
            scale_student,
        )
        row_start = 0 + offset
        top_teacher = jnp.max(teacher_logit, axis=1)
        top_student = jnp.max(student_logit, axis=1)
        teacher_row_peak = lax.dynamic_update_slice_in_dim(
            teacher_row_peak, top_teacher, row_start, 0
        )
        student_row_peak = lax.dynamic_update_slice_in_dim(
            student_row_peak, top_student, row_start, 0
        )
        teacher_row_total = lax.dynamic_update_slice_in_dim(
            teacher_row_total,
            jnp.sum(jnp.exp(teacher_logit - top_teacher[:, None]), axis=1),
            row_start,
            0,
        )
        student_row_total = lax.dynamic_update_slice_in_dim(
            student_row_total,
            jnp.sum(jnp.exp(student_logit - top_student[:, None]), axis=1),
            row_start,
            0,
        )
        teacher_column_peak, teacher_column_total = fold_columns(
            teacher_column_peak, teacher_column_total, teacher_logit
        )
        student_column_peak, student_column_total = fold_columns(
            student_column_peak, student_column_total, student_logit
        )
    local_stats = (
        teacher_row_peak,
        teacher_row_total,
        student_row_peak,
        student_row_total,
        teacher_column_peak,
        teacher_column_total,
        student_column_peak,
        student_column_total,
    )
    (
        teacher_row_peak,
        teacher_row_total,
        student_row_peak,
        student_row_total,
        teacher_column_peak,
        teacher_column_total,
        student_column_peak,
        student_column_total,
    ) = local_stats
    row_top_teacher, row_top_student = lax.pmax((teacher_row_peak, student_row_peak), "txt")
    row_sum_teacher, row_sum_student = lax.psum(
        (
            teacher_row_total * jnp.exp(teacher_row_peak - row_top_teacher),
            student_row_total * jnp.exp(student_row_peak - row_top_student),
        ),
        "txt",
    )
    column_top_teacher, column_top_student = lax.pmax(
        (teacher_column_peak, student_column_peak), "img"
    )
    column_sum_teacher, column_sum_student = lax.psum(
        (
            teacher_column_total * jnp.exp(teacher_column_peak - column_top_teacher),
            student_column_total * jnp.exp(student_column_peak - column_top_student),
        ),
        "img",
    )
    teacher_row_lse = row_top_teacher + jnp.log(row_sum_teacher)
    student_row_lse = row_top_student + jnp.log(row_sum_student)
    teacher_column_lse = column_top_teacher + jnp.log(column_sum_teacher)
    student_column_lse = column_top_student + jnp.log(column_sum_student)
    pieces = (image_teacher, image_student)
    image_total = jnp.zeros((tile_rows, student_image.shape[1]), jnp.float32)
    text_total = jnp.zeros((tile_cols, student_image.shape[1]), jnp.float32)
    divergence = jnp.zeros((), jnp.float32)
    for offset, count in row_blocks(pieces[0].shape[0]):
        block_student = pieces[1][offset : offset + count]
        teacher_logit, student_logit = pair_logits(
            pieces[0][offset : offset + count],
            block_student,
            text_teacher,
            text_student,
            scale_teacher,
            scale_student,
        )
        row_start = 0 + offset
        lse_teacher = lax.dynamic_slice_in_dim(teacher_row_lse, row_start, count)
        lse_student = lax.dynamic_slice_in_dim(student_row_lse, row_start, count)
        teacher_row_prob = jnp.exp(teacher_logit - lse_teacher[:, None])
        student_row_prob = jnp.exp(student_logit - lse_student[:, None])
        teacher_column_prob = jnp.exp(teacher_logit - teacher_column_lse[None, :])
        student_column_prob = jnp.exp(student_logit - student_column_lse[None, :])
        difference = teacher_logit - student_logit
        divergence = (
            divergence
            + jnp.sum(teacher_row_prob * difference)
            + jnp.sum(teacher_column_prob * difference)
        )
        delta = student_row_prob - teacher_row_prob + (student_column_prob - teacher_column_prob)
        delta_high, delta_low = split_delta(delta)
        image_part = jnp.dot(
            delta_high, text_student, preferred_element_type=jnp.float32
        ) + jnp.dot(delta_low, text_student, preferred_element_type=jnp.float32)
        image_total = lax.dynamic_update_slice_in_dim(image_total, image_part, row_start, 0)
        text_total = (
            text_total
            + jnp.einsum("rc,rd->cd", delta_high, block_student, preferred_element_type=jnp.float32)
            + jnp.einsum("rc,rd->cd", delta_low, block_student, preferred_element_type=jnp.float32)
        )
    image_total, text_total, divergence = (image_total, text_total, divergence)
    row_share = teacher_image.shape[0]
    column_share = teacher_text.shape[0]
    row_gap = jnp.sum(
        lax.dynamic_slice_in_dim(
            student_row_lse - teacher_row_lse, lax.axis_index("txt") * row_share, row_share
        )
    )
    column_gap = jnp.sum(
        lax.dynamic_slice_in_dim(
            student_column_lse - teacher_column_lse,
            lax.axis_index("img") * column_share,
            column_share,
        )
    )
    total = lax.psum(divergence + row_gap + column_gap, ("img", "txt"))
    pair_count = tile_rows * lax.axis_size("img")
    loss = total / (2.0 * pair_count)
    image_grad = (
        lax.psum_scatter(image_total, "txt", scatter_dimension=0, tiled=True) * scale_student
    )
    text_grad = lax.psum_scatter(text_total, "img", scatter_dimension=0, tiled=True) * scale_student
    return (loss, image_grad, text_grad)


def solution(mesh):
    in_specs = (
        P(("img", "txt"), None),
        P(("txt", "img"), None),
        P(("img", "txt"), None),
        P(("txt", "img"), None),
    )
    out_specs = (P(), P(("img", "txt"), None), P(("txt", "img"), None))
    return jax.shard_map(local, mesh=mesh, in_specs=in_specs, out_specs=out_specs, check_vma=False)
```

profile of v0, /device:TPU:1, one launch (start us, length us, event | category | flops | bytes accessed | tf_op | source)
XLA Modules:
  0.0 510.8 jit_solution(6822559462705897796)
XLA Ops:
  10.0 27.0 %all-gather.11.cloned.1.call-done = bf16[1024,512]{1,0:T(8,128)(2,1)} async-done(((bf16[128,512]{1,0:T(8,128)(2,1)}), bf16[1024,512]{1,0:T(8,128)(2,1)}) %all-gather.11.cloned.1.call-update) | async-done | bytes 1048592 | tf_op jit(solution)/shard_map/all_gather | solution.py:48
  37.0 45.6 %all-gather.9.cloned.1.call-done = bf16[2048,512]{1,0:T(8,128)(2,1)} async-done(((bf16[128,512]{1,0:T(8,128)(2,1)}), bf16[2048,512]{1,0:T(8,128)(2,1)}) %all-gather.9.cloned.1.call-update) | async-done | bytes 2097168 | tf_op jit(solution)/shard_map/all_gather | solution.py:57
  82.6 2.4 fusion.46
  84.9 0.8 fusion.47
  85.8 0.9 fusion.29
  88.8 0.9 fusion.27
  90.2 21.1 %all-gather.7.cloned.1.call-done = bf16[1024,1280]{1,0:T(8,128)(2,1)} async-done(((bf16[128,1280]{1,0:T(8,128)(2,1)}), bf16[1024,1280]{1,0:T(8,128)(2,1)}) %all-gather.7.cloned.1.call-update) | async-done | bytes 2621456 | tf_op jit(solution)/shard_map/all_gather | solution.py:47
  111.3 58.3 %all-gather.5.cloned.1.call-done = bf16[2048,1280]{1,0:T(8,128)(2,1)} async-done(((bf16[128,1280]{1,0:T(8,128)(2,1)}), bf16[2048,1280]{1,0:T(8,128)(2,1)}) %all-gather.5.cloned.1.call-update) | async-done | bytes 5242896 | tf_op jit(solution)/shard_map/all_gather | solution.py:56
  169.6 5.1 %fusion.34 = (f32[1024]{0:T(1024)S(1)}, f32[512]{0:T(512)S(1)}, f32[512,1024]{1,0:T(8,128)}) fusion(bf16[1024,1280]{1,0:T(8,128)(2,1)} %all-gather.7.cloned.1.call-done, bf16[2048,1280]{1,0:T(8,128)(2,1)} %all-gather.5.cloned.1.call-done), kind=kOutput, calls=%fused_computation.111 | convolution fusion | flops 1343748608 | bytes 6035456 | tf_op jit(solution)/shard_map/rd,cd->rc/dot_general | solution.py:13
  174.7 2.9 fusion.31
  177.6 2.8 fusion.32
  180.5 2.9 fusion.33
  183.4 12.8 %all-reduce.7 = (f32[1024]{0:T(1024)S(1)}, f32[1024]{0:T(1024)S(1)}) all-reduce(f32[1024]{0:T(1024)S(1)} %get-tuple-element.67, f32[1024]{0:T(1024)S(1)} %get-tuple-element.64), channel_id=1, replica_groups=mesh['img'=8,'txt'=16] {'img'}, use_global_device_ids=true, to_apply=%region_15.0 | all-reduce | flops 2048 | bytes 16384 | tf_op jit(solution)/shard_map/pmax | solution.py:132
  196.2 3.9 exponential_reduce_fusion.10
  200.1 1.7 exponential_reduce_fusion.8
  201.8 14.9 %psum.36 = f32[1024]{0:T(1024)S(1)} all-reduce(f32[1024]{0:T(1024)S(1)} %exponential_multiply_fusion.3), channel_id=1, replica_groups=mesh['img'=8,'txt'=16] {'img'}, use_global_device_ids=true, to_apply=%region_20.0 | all-reduce | flops 1024 | bytes 8192 | tf_op jit(solution)/shard_map/psum | solution.py:135
  216.8 58.5 %all-reduce.6 = (f32[2048]{0:T(1024)S(1)}, f32[2048]{0:T(1024)S(1)}) all-reduce(f32[2048]{0:T(1024)S(1)} %constant_dynamic-update-slice_fusion.3, f32[2048]{0:T(1024)S(1)} %constant_dynamic-update-slice_fusion.1), channel_id=1, replica_groups=mesh['img'=8,'txt'=16] {'txt'}, use_global_device_ids=true, to_apply=%region_4.0 | all-reduce | flops 4096 | bytes 32768 | tf_op jit(solution)/shard_map/pmax | solution.py:124
  275.4 55.6 %all-reduce.5 = (f32[2048]{0:T(1024)S(1)}, f32[2048]{0:T(1024)S(1)}) all-reduce(f32[2048]{0:T(1024)S(1)} %exponential_multiply_fusion.1, f32[2048]{0:T(1024)S(1)} %exponential_multiply_fusion), channel_id=1, replica_groups=mesh['img'=8,'txt'=16] {'txt'}, use_global_device_ids=true, to_apply=%region_9.0 | all-reduce | flops 4096 | bytes 32768 | tf_op jit(solution)/shard_map/psum | solution.py:125
  331.0 8.4 %multiply_reduce_fusion = (f32[]{:T(128)}, f32[]{:T(128)}, f32[1024]{0:T(1024)S(1)}, f32[1024]{0:T(1024)S(1)}, f32[]{:T(128)}, /*index=5*/f32[]{:T(128)}, f32[10...) fusion(f32[512,1024]{1,0:T(8,128)} %get-tuple-element.84, ...), kind=kLoop, calls=%fused_computation.17 | loop fusion | flops 18870264 | bytes 16822304 | tf_op jit(solution)/shard_map/reduce_sum | solution.py:171
  339.5 40.2 %psum.38 = f32[1024]{0:T(1024)S(1)} all-reduce(f32[1024]{0:T(1024)S(1)} %exponential_multiply_fusion.2), channel_id=1, replica_groups=mesh['img'=8,'txt'=16] {'img'}, use_global_device_ids=true, to_apply=%region_48.0 | all-reduce | flops 1024 | bytes 8192 | tf_op jit(solution)/shard_map/psum | solution.py:135
  379.7 7.8 %fusion.35 = (bf16[512,1024]{1,0:T(8,128)(2,1)S(1)}, f32[512,1024]{1,0:T(8,128)S(1)}, bf16[512,1024]{1,0:T(8,128)(2,1)S(1)}, f32[512,1024]{1,0:T(8,128)S(1)}, bf...) fusion(f32[512,1024]{1,0:T(8,128)} %get-tuple-element.84, ...), kind=kLoop, calls=%fused_computation.112 | loop fusion | flops 16777216 | bytes 29384704 | tf_op jit(solution)/shard_map/convert_element_type | solution.py:32
  393.0 2.7 add_add_fusion
  396.1 2.1 fusion.48
  398.9 2.5 dynamic_update_slice.76
  404.6 0.9 copy-done.13
  405.5 1.8 fusion.2
  407.3 1.7 fusion.1
  409.0 1.7 fusion
  418.5 62.5 %psum.39 = f32[]{:T(128)} all-reduce(f32[]{:T(128)S(6)} %add.160), channel_id=1, replica_groups=mesh['img'=8,'txt'=16] {'img','txt'}, use_global_device_ids=true, to_apply=%region_50.0 | all-reduce | flops 1 | bytes 8 | tf_op jit(solution)/shard_map/psum | solution.py:199
  481.7 1.7 broadcast_multiply_fusion
  483.4 17.8 %reduce-scatter.3.cloned.1.call-done = f32[128,512]{1,0:T(8,128)} async-done(((f32[2048,512]{1,0:T(8,128)}), f32[128,512]{1,0:T(8,128)}) %reduce-scatter.3.cloned.1.call-update) | async-done | bytes 262160 | tf_op jit(solution)/shard_map/reduce_scatter | solution.py:203
  501.2 1.7 broadcast_multiply_fusion.1
  (107 shorter events, 16.4 us)
Async XLA Ops:
  7.2 29.8 %all-gather.11.cloned.1.call-start = ((), (), s32[]{:S(2)}) async-start(), calls=%async_computation.5 | async-start | bytes 1179648 | tf_op jit(solution)/shard_map/all_gather | solution.py:48
  7.9 74.7 %all-gather.9.cloned.1.call-start = ((), (), s32[]{:S(2)}) async-start(), calls=%async_computation.4 | async-start | bytes 2228224 | tf_op jit(solution)/shard_map/all_gather | solution.py:57
  8.6 102.6 %all-gather.7.cloned.1.call-start = ((), (), s32[]{:S(2)}) async-start(), calls=%async_computation.3 | async-start | bytes 2949120 | tf_op jit(solution)/shard_map/all_gather | solution.py:47
  9.4 160.2 %all-gather.5.cloned.1.call-start = ((), (), s32[]{:S(2)}) async-start(), calls=%async_computation.2 | async-start | bytes 5570560 | tf_op jit(solution)/shard_map/all_gather | solution.py:56
  10.0 471.7 %reduce-scatter.5.cloned.1.call-start = ((), (), s32[]{:S(2)}) async-start(), calls=%async_computation.7 | async-start | bytes 2359296 | tf_op jit(solution)/shard_map/reduce_scatter | solution.py:205
  37.0 48.0 %copy-start = (bf16[1024,512]{1,0:T(8,128)(2,1)S(1)}, bf16[1024,512]{1,0:T(8,128)(2,1)}, u32[]{:S(2)}) copy-start(bf16[1024,512]{1,0:T(8,128)(2,1)} %all-gather.11.cloned.1.call-done) | copy-start | bytes 3145732
  82.6 2.4 copy-start.4
  85.8 1.3 copy-start.1
  87.9 1.8 copy-start.2
  88.8 1.4 copy-start.3
  169.6 5.2 %copy-start.24 = (bf16[2048,1280]{1,0:T(8,128)(2,1)S(1)}, bf16[2048,1280]{1,0:T(8,128)(2,1)}, u32[]{:S(2)}) copy-start(bf16[2048,1280]{1,0:T(8,128)(2,1)} %all-gather.5.cloned.1.call-done) | copy-start | bytes 15728644
  169.6 5.2 %copy-start.25 = (bf16[1024,1280]{1,0:T(8,128)(2,1)S(1)}, bf16[1024,1280]{1,0:T(8,128)(2,1)}, u32[]{:S(2)}) copy-start(bf16[1024,1280]{1,0:T(8,128)(2,1)} %all-gather.7.cloned.1.call-done) | copy-start | bytes 7864324
  196.2 4.0 copy-start.8
  196.2 4.0 copy-start.9
  379.7 7.9 %copy-start.5 = (bf16[2048,512]{1,0:T(8,128)(2,1)S(1)}, bf16[2048,512]{1,0:T(8,128)(2,1)}, u32[]{:S(2)}) copy-start(bf16[2048,512]{1,0:T(8,128)(2,1)} %all-gather.9.cloned.1.call-done) | copy-start | bytes 6291460
  387.6 3.1 copy-start.10
  387.6 3.1 copy-start.18
  387.6 3.8 copy-start.12
  387.6 3.8 copy-start.20
  387.6 4.6 copy-start.14
  387.6 4.6 copy-start.22
  387.6 5.4 %copy-start.6 = (f32[512,1024]{1,0:T(8,128)}, f32[512,1024]{1,0:T(8,128)S(1)}, u32[]{:S(2)}) copy-start(f32[512,1024]{1,0:T(8,128)S(1)} %get-tuple-element.55) | copy-start | bytes 6291460
  387.6 5.4 %copy-start.16 = (bf16[512,1024]{1,0:T(8,128)(2,1)}, bf16[512,1024]{1,0:T(8,128)(2,1)S(1)}, u32[]{:S(2)}) copy-start(bf16[512,1024]{1,0:T(8,128)(2,1)S(1)} %get-tuple-element.54) | copy-start | bytes 3145732
  395.8 2.4 copy-start.15
  395.8 105.4 %reduce-scatter.3.cloned.1.call-start = ((), (), s32[]{:S(2)}) async-start(), calls=%async_computation.6 | async-start | bytes 4456448 | tf_op jit(solution)/shard_map/reduce_scatter | solution.py:203
  396.0 2.1 copy-start.23
  398.9 2.5 copy-start.21
  401.4 1.2 copy-start.19
  402.6 1.2 copy-start.17
  403.9 1.6 copy-start.13
  405.5 1.8 copy-start.11
  407.3 1.7 copy-start.7
Sparse Core Ops, SparseCore 0:
  9.7 27.2 all-gather.10
  39.1 43.4 all-gather.8
  84.2 26.9 all-gather.6
  113.3 56.2 all-gather.4
  395.9 24.0 reduce-scatter.4
  423.1 77.9 reduce-scatter.2
where the time goes:
time: 512 us; the launch traced here: 511 us
  blocking collectives  244 us (48%)
  waiting for transfers between devices  172 us (34%)
  matrix products  36.8 us (7%)
  other arithmetic  28.5 us (6%)
  between operations  22.8 us (4%)
  local copies, waits for them, and re-layouts  5.47 us (1%)
    psum x1, blocking collectives, local(): total = lax.psum(divergence + row_gap + column_gap, ('img', 'txt'))  62.5 us
    pmax x1, blocking collectives, local(): lax.pmax((teacher_row_peak, student_row_peak), 'txt')  58.5 us
    all_gather x1, waiting for transfers between devices, local(): lax.all_gather(teacher_image, 'txt', axis=0, tiled=True)  58.3 us
    psum x1, blocking collectives, local(): lax.psum((teacher_row_total * jnp.exp(teacher_row_peak - row_top_teacher)...  55.6 us
    psum x2, blocking collectives, local(): lax.psum((teacher_column_total * jnp.exp(teacher_column_peak - column_top...  55.1 us
    all_gather x1, waiting for transfers between devices, local(): lax.all_gather(student_image, 'txt', axis=0, tiled=True)  45.6 us
    all_gather x1, waiting for transfers between devices, local(): lax.all_gather(student_text, 'img', axis=0, tiled=True)  27 us
    all_gather x1, waiting for transfers between devices, local(): lax.all_gather(teacher_text, 'img', axis=0, tiled=True)  21.1 us
  transfers between devices with their start and end apart: 6, of which 5 were waited for; matrix products, arithmetic and copies ran while one was open for 4% of the time, Pallas kernels for 0%

commit v1 on v0

v1 whole, which is shorter than its diff:
```python
import functools
import math

import jax
import jax.numpy as jnp
from jax import lax
from jax.experimental import pallas as pl
from jax.experimental.pallas import tpu as pltpu
from jax.sharding import PartitionSpec as P

MESH = pl.DeviceIdType.MESH
F32 = jnp.float32
BF16 = jnp.bfloat16
UNIT = 128
TW = 1280
SW = 512
W = TW + SW
NI = 8
NP = 8
FIRST = 5
LOG2E = 1.4426950408889634
LN2 = 0.6931471805599453
LOW = -1e30
CODE = 2.0**18
TINY = 1e-25


def inv(k):
    return (k // 4) * 4 + (4 - k % 4) % 4


def dot_nt(a, b):
    return lax.dot_general(a, b, (((1,), (1,)), ((), ())), preferred_element_type=F32)


def encode(v):
    v2 = v * v
    return (v2 * v2 * v).astype(BF16)


def decode(code):
    y = code.astype(F32)
    u = jnp.exp2(jnp.log2(jnp.abs(y)) * 0.2)
    return jnp.where(y < 0.0, -u, u)


def log_sum(peak, total):
    return peak + jnp.log2(total)


def kernel(
    pairs,
    ti, tt, si, st,
    loss_o, ig_o, tg_o,
    img, txt, lt, ls, rm, rs, cm, cs, d, ist,
    rmsg, cmsg, rrx, crx, rlse, clse,
    isend, irecv, xsend, xrecv, keep, tsend, trecv,
    lsend, lrx_i, lrx_t,
    lsem, ssem, rsem,
):
    i_index, t_index = lax.axis_index("img"), lax.axis_index("txt")
    z, c, x, y = i_index // 2, i_index % 2, t_index // 4, t_index % 4
    xa = x + 1 - 2 * (x % 2)
    xb = 3 - x

    def i_peer(k):
        return (z * 2 + c, (xa if k // 4 else x) * 4 + (y + k % 4) % 4)

    def t_peer(cc, k):
        return (((z + k % 4) % 4) * 2 + (c + cc) % 2, (xb if k // 4 else x) * 4 + y)

    serial = [0]
    begun = []

    def send(src, dst, device):
        n = serial[0]
        serial[0] += 1
        copy = pltpu.make_async_remote_copy(
            src_ref=src, dst_ref=dst, send_sem=ssem.at[n], recv_sem=rsem.at[n],
            device_id=device, device_id_type=MESH,
        )
        copy.start()
        begun.append(copy)
        return copy

    loads = [
        pltpu.make_async_copy(ti, img.at[0, :, 0:TW], lsem.at[0]),
        pltpu.make_async_copy(si, img.at[0, :, TW:W], lsem.at[1]),
        pltpu.make_async_copy(tt, txt.at[0, :, 0:TW], lsem.at[2]),
        pltpu.make_async_copy(st, txt.at[0, :, TW:W], lsem.at[3]),
    ]
    for copy in loads:
        copy.start()
    barrier = pltpu.get_barrier_semaphore()
    for k in range(1, 8):
        pl.semaphore_signal(barrier, inc=1, device_id=i_peer(k), device_id_type=MESH)
    for j in range(1, 16):
        pl.semaphore_signal(barrier, inc=1, device_id=t_peer(j % 2, j // 2), device_id_type=MESH)
    rm[...] = jnp.full(rm.shape, LOW, F32)
    rs[...] = jnp.zeros(rs.shape, F32)
    cm[...] = jnp.full(cm.shape, LOW, F32)
    cs[...] = jnp.zeros(cs.shape, F32)
    pl.semaphore_wait(barrier, 22)
    for copy in loads:
        copy.wait()

    def image_at(k, half=None):
        return img.at[k] if half is None else img.at[k, pl.ds(half * 64, 64)]

    def text_at(k, half=None):
        return txt.at[2 * k] if half is None else txt.at[2 * k, pl.ds(half * 64, 64)]

    sides = ((image_at, i_peer, False), (text_at, functools.partial(t_peer, 0), True))
    crossings = []

    def cross(k):
        crossings.append(send(txt.at[2 * k], txt.at[2 * k + 1], t_peer(1, 0)))

    flight = []
    for at, peer, _ in sides:
        flight.append(
            dict(
                plus=send(at(0), at(3), peer(1)),
                minus=send(at(0), at(1), peer(3)),
                side=send(at(0), at(4), peer(4)),
            )
        )
    cross(0)
    for (at, peer, is_text), f in zip(sides, flight):
        f["minus"].wait_recv()
        f["far_minus"] = send(at(1, 0), at(2, 0), peer(3))
        f["plus"].wait_recv()
        f["far_plus"] = send(at(3, 1), at(2, 1), peer(1))
        if is_text:
            cross(1)
            cross(3)
    for (at, peer, is_text), f in zip(sides, flight):
        f["side"].wait_recv()
        f["side_plus"] = send(at(4), at(7), peer(1))
        f["side_minus"] = send(at(4), at(5), peer(3))
        if is_text:
            cross(4)
    for (at, peer, is_text), f in zip(sides, flight):
        f["far_minus"].wait_recv()
        f["far_plus"].wait_recv()
        f["side_far"] = send(at(2), at(6), peer(4))
        if is_text:
            cross(2)
    for copy in crossings:
        copy.wait_recv()
    crossings.clear()

    scale_t = LOG2E * TW**-0.5
    scale_s = LOG2E * SW**-0.5

    def fold(model, logit, p, u):
        rows = pl.ds(u * UNIT, UNIT)
        left, right = logit[p, rows, 0:128], logit[p, rows, 128:256]
        old = rm[model, rows, :]
        new = jnp.maximum(old, jnp.maximum(left, right))
        rm[model, rows, :] = new
        rs[model, rows, :] = (
            rs[model, rows, :] * jnp.exp2(old - new) + jnp.exp2(left - new) + jnp.exp2(right - new)
        )
        for h, part in ((0, left), (1, right)):
            lanes = slice(h * 128, h * 128 + 128)
            part = part.reshape(16, 8, 128)
            old = cm[model, p, :, lanes]
            new = jnp.maximum(old, jnp.max(part, axis=0))
            cm[model, p, :, lanes] = new
            cs[model, p, :, lanes] = cs[model, p, :, lanes] * jnp.exp2(old - new) + jnp.sum(
                jnp.exp2(part - new[None]), axis=0
            )

    def block(p, u0, count):
        rows = slice(u0 * UNIT, (u0 + count) * UNIT)
        both = pl.ds(p * 2, 2)
        lt[p, rows, :] = scale_t * dot_nt(
            img[u0 : u0 + count, :, 0:TW].reshape(count * UNIT, TW),
            txt[both, :, 0:TW].reshape(2 * UNIT, TW),
        )
        ls[p, rows, :] = scale_s * dot_nt(
            img[u0 : u0 + count, :, TW:W].reshape(count * UNIT, SW),
            txt[both, :, TW:W].reshape(2 * UNIT, SW),
        )

        @pl.loop(u0, u0 + count)
        def _(u):
            fold(0, lt, p, u)
            fold(1, ls, p, u)

    @pl.loop(0, FIRST)
    def _(p):
        block(p, 0, FIRST)

    for (at, peer, is_text), f in zip(sides, flight):
        f["side_plus"].wait_recv()
        f["side_minus"].wait_recv()
        if is_text:
            cross(5)
            cross(7)
        f["side_far"].wait_recv()
        if is_text:
            cross(6)
    for copy in crossings:
        copy.wait_recv()

    @pl.loop(0, FIRST)
    def _(p):
        block(p, FIRST, NI - FIRST)

    @pl.loop(FIRST, NP)
    def _(p):
        block(p, 0, 4)
        block(p, 4, 4)

    def largest(ref, count):
        def step(n, best):
            part = jnp.abs(ref[n, :, TW:W].astype(F32)).reshape(16, 8, SW)
            return jnp.maximum(best, jnp.max(part, axis=0))

        best = lax.fori_loop(0, count, step, jnp.zeros((8, SW), F32))
        return jnp.broadcast_to(jnp.max(best, axis=(0, 1), keepdims=True), (1, 128))

    image_top = jnp.maximum(largest(img, NI), TINY)
    text_top = jnp.maximum(largest(txt, 2 * NP), TINY)

    @pl.loop(0, NI)
    def _(u):
        rows = pl.ds(pl.multiple_of(u * UNIT, UNIT), UNIT)
        for model in range(2):
            peaks = rm[model, rows, :].T
            totals = rs[model, rows, :].T
            peak = jnp.max(peaks, axis=0, keepdims=True)
            total = jnp.sum(totals * jnp.exp2(peaks - peak), axis=0, keepdims=True)
            rmsg[u, model : model + 1, :] = log_sum(peak, total)
        rmsg[u, 2:8, :] = jnp.zeros((6, 128), F32)

    @pl.loop(0, NP)
    def _(p):
        for model in range(2):
            peaks = cm[model, p]
            peak = jnp.max(peaks, axis=0, keepdims=True)
            total = jnp.sum(cs[model, p] * jnp.exp2(peaks - peak), axis=0, keepdims=True)
            lse = log_sum(peak, total)
            for h in range(2):
                cmsg[2 * p + h, model : model + 1, :] = lse[:, h * 128 : h * 128 + 128]
        for h in range(2):
            cmsg[2 * p + h, 2:3, :] = image_top
            cmsg[2 * p + h, 3:8, :] = jnp.zeros((5, 128), F32)

    parts = [send(rmsg.at[k], rrx.at[inv(k)], i_peer(k)) for k in range(1, 8)]
    parts += [
        send(cmsg.at[j], crx.at[2 * inv(j // 2) + j % 2], t_peer(j % 2, j // 2))
        for j in range(1, 16)
    ]
    for block_index in range(NI // 2):
        turned = img[2 * block_index : 2 * block_index + 2, :, TW:W].reshape(2 * UNIT, SW).T
        ist[:, block_index * 512 : block_index * 512 + 256] = turned
        ist[:, block_index * 512 + 256 : block_index * 512 + 512] = turned
    for copy in parts:
        copy.wait_recv()

    def combine(own, received, count):
        peak = own
        for k in range(1, count):
            peak = jnp.maximum(peak, received[k])
        total = jnp.exp2(own - peak)
        for k in range(1, count):
            total = total + jnp.exp2(received[k] - peak)
        return log_sum(peak, total)

    chip_top = jnp.maximum(image_top, crx[1, 2:3, :])
    rlse[0] = combine(rmsg[0], rrx, 8)
    rlse[0, 2:3, :] = text_top
    clse[0] = combine(cmsg[0], crx, 16)
    clse[0, 2:3, :] = chip_top
    parts = [send(rlse.at[0], rlse.at[inv(k)], i_peer(k)) for k in range(1, 8)]
    parts += [
        send(clse.at[0], clse.at[2 * inv(j // 2) + j % 2], t_peer(j % 2, j // 2))
        for j in range(1, 16)
    ]
    gap = (rlse[0, 1:2, :] - rlse[0, 0:1, :]) + (clse[0, 1:2, :] - clse[0, 0:1, :])
    for copy in parts:
        copy.wait_recv()

    image_code = CODE * SW**-0.5 / text_top[0:1, 0:1]
    text_code = CODE * SW**-0.5 / chip_top[0:1, 0:1]
    grad_flights = []
    diverge = jnp.zeros((8, 128), F32)
    for b in (3, 1, 2, 0):
        rows = slice(b * 256, b * 256 + 256)
        lse_t, lse_s = (
            jnp.concatenate(
                [
                    jnp.broadcast_to(rlse[2 * b + h, model : model + 1, :], (128, 128)).T
                    for h in range(2)
                ],
                axis=0,
            )
            for model in range(2)
        )

        def step(p, carry, b=b, rows=rows, lse_t=lse_t, lse_s=lse_s):
            total, diverge = carry
            for h in range(2):
                lanes = slice(h * 128, h * 128 + 128)
                t = lt[p, rows, lanes]
                s = ls[p, rows, lanes]
                j = 2 * p + h
                teacher = jnp.exp2(t - lse_t) + jnp.exp2(t - clse[j, 0:1, :])
                student = jnp.exp2(s - lse_s) + jnp.exp2(s - clse[j, 1:2, :])
                diverge = diverge + jnp.sum((teacher * (t - s)).reshape(32, 8, 128), axis=0)
                delta = student - teacher
                high = delta.astype(BF16)
                low = (delta - high.astype(F32)).astype(BF16)
                d[p, b, 0:256, lanes] = high
                d[p, b, 256:512, lanes] = low
            weights = txt[pl.ds(2 * p, 2), :, TW:W].reshape(2 * UNIT, SW)
            total = total + jnp.dot(d[p, b], weights, preferred_element_type=F32)
            return total, diverge

        total, diverge = lax.fori_loop(0, NP, step, (jnp.zeros((512, SW), F32), diverge))
        total = total[0:256] + total[256:512]
        for h in (1, 0):
            k = 2 * b + h
            part = total[h * 128 : h * 128 + 128]
            if k == 0:
                ig_o[...] = part * SW**-0.5
            else:
                isend[k] = encode(part * image_code)
                grad_flights.append(send(isend.at[k], irecv.at[inv(k)], i_peer(k)))

    first_row = lax.broadcasted_iota(jnp.int32, (8, 128), 0) == 0
    lsend[0] = diverge + jnp.where(first_row, jnp.broadcast_to(gap, (8, 128)), 0.0)
    loss_flights = [send(lsend.at[0], lrx_i.at[inv(k)], i_peer(k)) for k in range(1, 8)]

    order = [6, 5, 7, 2, 1, 3, 4, 0]
    crossed = []

    def pass_on(k):
        crossed[order.index(k)].wait_recv()
        part = keep[k] + xrecv[k]
        if k == 0:
            keep[0] = part
        else:
            tsend[k] = encode(part * text_code)
            grad_flights.append(send(tsend.at[k], trecv.at[inv(k)], t_peer(0, k)))

    for n, k in enumerate(order):
        part = jnp.dot(ist[...], d[k].reshape(2048, 256), preferred_element_type=F32)
        keep[k] = part[:, 0:128]
        xsend[k] = part[:, 128:256]
        crossed.append(send(xsend.at[k], xrecv.at[k], t_peer(1, 0)))
        if n >= 1:
            pass_on(order[n - 1])
        if n == 4:
            for copy in loss_flights:
                copy.wait_recv()
            loss_part = lsend[0]
            for q in range(1, 8):
                loss_part = loss_part + lrx_i[q]
            lsend[1] = loss_part
            loss_flights = [
                send(lsend.at[1], lrx_t.at[2 * inv(j // 2) + j % 2], t_peer(j % 2, j // 2))
                for j in range(1, 16)
            ]
    pass_on(order[-1])

    for copy in loss_flights:
        copy.wait_recv()
    loss_part = lsend[1]
    for q in range(1, 16):
        loss_part = loss_part + lrx_t[q]
    loss = jnp.sum(loss_part, axis=(0, 1), keepdims=True) * (LN2 / (2.0 * pairs))
    loss_o[...] = jnp.broadcast_to(loss, (8, 128))

    for copy in grad_flights:
        copy.wait_recv()
    image_total = ig_o[...]
    for k in range(1, 8):
        image_total = image_total + decode(irecv[k]) * (rlse[k, 2:3, 0:1] * (1.0 / CODE))
    ig_o[...] = image_total
    text_total = keep[0] * SW**-0.5
    for k in range(1, 8):
        text_total = text_total + decode(trecv[k]) * (clse[2 * k, 2:3, 0:1] * (1.0 / CODE))
    tg_o[...] = text_total.T
    for copy in begun:
        copy.wait_send()


def local(teacher_image, teacher_text, student_image, student_text):
    pairs = teacher_image.shape[0] * lax.axis_size("img") * lax.axis_size("txt")
    vmem = pltpu.VMEM
    loss, image_grad, text_grad = pl.pallas_call(
        functools.partial(kernel, pairs),
        out_shape=(
            jax.ShapeDtypeStruct((8, 128), F32),
            jax.ShapeDtypeStruct((UNIT, SW), F32),
            jax.ShapeDtypeStruct((UNIT, SW), F32),
        ),
        in_specs=[pl.BlockSpec(memory_space=pl.ANY)] * 4,
        out_specs=[pl.BlockSpec(memory_space=vmem)] * 3,
        scratch_shapes=[
            vmem((NI, UNIT, W), BF16),
            vmem((2 * NP, UNIT, W), BF16),
            vmem((NP, NI * UNIT, 256), F32),
            vmem((NP, NI * UNIT, 256), F32),
            vmem((2, NI * UNIT, 128), F32),
            vmem((2, NI * UNIT, 128), F32),
            vmem((2, NP, 8, 256), F32),
            vmem((2, NP, 8, 256), F32),
            vmem((NP, NI // 2, 512, 256), BF16),
            vmem((SW, 2 * NI * UNIT), BF16),
            vmem((8, 8, 128), F32),
            vmem((16, 8, 128), F32),
            vmem((8, 8, 128), F32),
            vmem((16, 8, 128), F32),
            vmem((8, 8, 128), F32),
            vmem((16, 8, 128), F32),
            vmem((8, UNIT, SW), BF16),
            vmem((8, UNIT, SW), BF16),
            vmem((8, SW, UNIT), F32),
            vmem((8, SW, UNIT), F32),
            vmem((8, SW, UNIT), F32),
            vmem((8, SW, UNIT), BF16),
            vmem((8, SW, UNIT), BF16),
            vmem((2, 8, 128), F32),
            vmem((8, 8, 128), F32),
            vmem((16, 8, 128), F32),
            pltpu.SemaphoreType.DMA((4,)),
            pltpu.SemaphoreType.DMA((128,)),
            pltpu.SemaphoreType.DMA((128,)),
        ],
        compiler_params=pltpu.CompilerParams(
            collective_id=0, has_side_effects=True, vmem_limit_bytes=62 * 2**20
        ),
        cost_estimate=pl.CostEstimate(
            flops=16_000_000_000, bytes_accessed=1_500_000, transcendentals=20_000_000
        ),
    )(teacher_image, teacher_text, student_image, student_text)
    return loss[0, 0], image_grad, text_grad


def solution(mesh):
    in_specs = (
        P(("img", "txt"), None),
        P(("txt", "img"), None),
        P(("img", "txt"), None),
        P(("txt", "img"), None),
    )
    out_specs = (P(), P(("img", "txt"), None), P(("txt", "img"), None))
    return jax.shard_map(local, mesh=mesh, in_specs=in_specs, out_specs=out_specs, check_vma=False)
```

time: 512 us -> 111 us (0.22)
  blocking collectives: 244 us -> 0 us
  waiting for transfers between devices: 172 us -> 0 us
  Pallas kernels: 0 us -> 106 us
  matrix products: 36.8 us -> 0 us
  other arithmetic: 28.5 us -> 0 us
  between operations: 22.8 us -> 0.64 us
    psum x4 -> x0, blocking collectives: 173 us -> none  [the longest x1 62.5 us: local(): total = lax.psum(divergence + row_gap + column_gap, ('img', 'txt'))]
    all_gather x4 -> x0, waiting for transfers between devices: 152 us -> none  [the longest x1 58.3 us: local(): lax.all_gather(teacher_image, 'txt', axis=0, tiled=True)]
    pallas_call x0 -> x1, Pallas kernels: none -> 106 us  [local(): pl.pallas_call(functools.partial(kernel, pairs), out_shape=(jax.ShapeDtyp...]
    pmax x2 -> x0, blocking collectives: 71.3 us -> none  [the longest x1 58.5 us: local(): lax.pmax((teacher_row_peak, student_row_peak), 'txt')]
    dot_general x24 -> x0, matrix products: 36.8 us -> none  [the longest x4 13.8 us: pair_logits(): jnp.einsum('rd,cd->rc', image_teacher, text_teacher, preferred_element_ty...]
    reduce_scatter x2 -> x0, waiting for transfers between devices: 17.8 us -> none  [the longest x1 17.8 us: local(): lax.psum_scatter(image_total, 'txt', scatter_dimension=0, tiled=True)]
    reduce_sum x5 -> x0, other arithmetic: 15.4 us -> none  [the longest x1 8.43 us: local(): jnp.sum(teacher_column_prob * difference)]
    convert_element_type x1 -> x0, other arithmetic: 7.83 us -> none  [split_delta(): delta_high = delta.astype(jnp.bfloat16)]
  transfers between devices with their start and end apart: 6 -> 0, of which waited for: 5 -> 0; matrix products, arithmetic and copies ran while one was open for 4% -> 0% of each run, Pallas kernels for 0% -> 0%
where the time goes in v1:
time: 111 us; the launch traced here: 110 us
  Pallas kernels  106 us (95%)
  local copies, waits for them, and re-layouts  3.61 us (3%)
    pallas_call x1, Pallas kernels, local(): pl.pallas_call(functools.partial(kernel, pairs), out_shape=(jax.ShapeDtyp...  106 us
    unnamed x4, local copies, waits for them, and re-layouts  2.42 us

profile of v1, /device:TPU:1, one launch (start us, length us, event | category | flops | bytes accessed | tf_op | source)
XLA Modules:
  0.0 110.4 jit_solution(4226403648962052034)
XLA Ops:
  0.6 106.1 %shard_map.67 = (f32[8,128]{1,0:T(8,128)}, f32[128,512]{1,0:T(8,128)}, f32[128,512]{1,0:T(8,128)}) custom-call(bf16[128,1280]{1,0:T(8,128)(2,1)} %ti.1, bf16[128,1280]{1,0:T(8,128)(2,1)} %tt.1, bf16[128,512]{1,0:T(8,128)(2,1)} %si.1, bf16[128,512]{1,0:T(8,128)(2,1)} %st.1), custom_call_target="tpu_custom_call" | custom-call | flops 16000000000 | bytes 1500000 | tf_op jit(solution)/shard_map/pallas_call | solution.py:395
  106.8 1.2 %slice.3 = f32[1,1]{1,0:T(1,128)} slice(f32[8,128]{1,0:T(8,128)} %get-tuple-element.6), slice={[0:1], [0:1]} | slice | bytes 8 | tf_op jit(solution)/shard_map/slice | solution.py:442
  108.0 0.0 copy-start
  108.0 1.7 %copy.9 = f32[128,512]{1,0:T(8,128)} copy(f32[128,512]{1,0:T(8,128)} %get-tuple-element.13) | data formatting | bytes 524288
  109.7 0.0 copy-done
  109.7 0.7 copy.10
Async XLA Ops:
  108.0 1.7 %copy-start = (f32[128,512]{1,0:T(8,128)S(1)}, f32[128,512]{1,0:T(8,128)}, u32[]{:S(2)}) copy-start(f32[128,512]{1,0:T(8,128)} %get-tuple-element.14) | copy-start | bytes 786436

commit v2 on v1

v2 whole, which is shorter than its diff:
```python
import functools
import math

import jax
import jax.numpy as jnp
from jax import lax
from jax.experimental import pallas as pl
from jax.experimental.pallas import tpu as pltpu
from jax.sharding import PartitionSpec as P

MESH = pl.DeviceIdType.MESH
F32 = jnp.float32
BF16 = jnp.bfloat16
UNIT = 128
TW = 1280
SW = 512
W = TW + SW
NI = 8
NP = 8
LOG2E = 1.4426950408889634
LN2 = 0.6931471805599453
LOW = -1e30
CODE = 2.0**18
TINY = 1e-25


SLOTS = ((0, 0), (0, 1), (0, 3), (1, 0), (0, 2), (1, 1), (1, 3), (1, 2))
BACK = tuple(SLOTS.index((a, (4 - r) % 4)) for a, r in SLOTS)


def dot_nt(a, b):
    return lax.dot_general(a, b, (((1,), (1,)), ((), ())), preferred_element_type=F32)


def encode(v):
    v2 = v * v
    return (v2 * v2 * v).astype(BF16)


def decode(code):
    y = code.astype(F32)
    u = jnp.exp2(jnp.log2(jnp.abs(y)) * 0.2)
    return jnp.where(y < 0.0, -u, u)


def log_sum(peak, total):
    return peak + jnp.log2(total)


def kernel(
    pairs,
    ti, tt, si, st,
    out,
    img, txt, lt, ls, rm, rs, cm, cs, d, ist,
    rmsg, cmsg, rrx, crx, rlse, clse,
    isend, irecv, xsend, xrecv, keep, tsend, trecv,
    lsend, lrx_i, lrx_t, top,
    lsem, ssem, rsem,
):
    i_index, t_index = lax.axis_index("img"), lax.axis_index("txt")
    z, c, x, y = i_index // 2, i_index % 2, t_index // 4, t_index % 4
    xa = x + 1 - 2 * (x % 2)
    xb = 3 - x

    def i_peer(slot):
        a, r = SLOTS[slot]
        return (z * 2 + c, (xa if a else x) * 4 + (y + r) % 4)

    def t_peer(cc, slot):
        a, r = SLOTS[slot]
        return (((z + r) % 4) * 2 + (c + cc) % 2, (xb if a else x) * 4 + y)

    serial = [0]
    begun = []

    def send(src, dst, device):
        n = serial[0]
        serial[0] += 1
        copy = pltpu.make_async_remote_copy(
            src_ref=src, dst_ref=dst, send_sem=ssem.at[n], recv_sem=rsem.at[n],
            device_id=device, device_id_type=MESH,
        )
        copy.start()
        begun.append(copy)
        return copy

    def arrived(copies):
        for copy in copies:
            copy.wait_recv()

    loads = [
        pltpu.make_async_copy(ti, img.at[0, :, 0:TW], lsem.at[0]),
        pltpu.make_async_copy(si, img.at[0, :, TW:W], lsem.at[1]),
        pltpu.make_async_copy(tt, txt.at[0, :, 0:TW], lsem.at[2]),
        pltpu.make_async_copy(st, txt.at[0, :, TW:W], lsem.at[3]),
    ]
    for copy in loads:
        copy.start()
    barrier = pltpu.get_barrier_semaphore()
    neighbours = [i_peer(q) for q in (1, 2, 3)] + [t_peer(0, q) for q in (1, 2, 3)] + [t_peer(1, 0)]
    for device in neighbours:
        pl.semaphore_signal(barrier, inc=1, device_id=device, device_id_type=MESH)
    rm[...] = jnp.full(rm.shape, LOW, F32)
    rs[...] = jnp.zeros(rs.shape, F32)
    cm[...] = jnp.full(cm.shape, LOW, F32)
    cs[...] = jnp.zeros(cs.shape, F32)
    pl.semaphore_wait(barrier, 7)
    for copy in loads:
        copy.wait()

    def image_at(slot, rows=(0, 128), columns=(0, W)):
        return img.at[slot, rows[0] : rows[1], columns[0] : columns[1]]

    def text_at(slot, rows=(0, 128), columns=(0, W)):
        return txt.at[2 * slot, rows[0] : rows[1], columns[0] : columns[1]]

    low_rows, high_rows = (0, 64), (64, 128)
    teacher_part, student_part = (0, TW), (TW, W)
    sides = ((image_at, i_peer), (text_at, functools.partial(t_peer, 0)))
    crossings = []

    def cross(slot, columns=(0, W)):
        part = slice(columns[0], columns[1])
        crossings.append(
            send(txt.at[2 * slot, :, part], txt.at[2 * slot + 1, :, part], t_peer(1, 0))
        )

    flights = [{} for _ in sides]
    for first, second in ((low_rows, high_rows), (high_rows, low_rows)):
        for (at, peer), f in zip(sides, flights):
            f["minus", first] = send(at(0, first), at(1, first), peer(2))
            f["plus", second] = send(at(0, second), at(2, second), peer(1))
            f["side", first] = send(at(0, first), at(3, first), peer(3))
    cross(0)
    for (at, peer), f in zip(sides, flights):
        f["minus", low_rows].wait_recv()
        f["far", low_rows] = send(at(1, low_rows), at(4, low_rows), peer(2))
    for (at, peer), f in zip(sides, flights):
        f["plus", high_rows].wait_recv()
        f["far", high_rows] = send(at(2, high_rows), at(4, high_rows), peer(1))
    for (at, peer), f in zip(sides, flights):
        arrived([f["side", low_rows], f["side", high_rows]])
        for part in (teacher_part, student_part):
            f["side_minus", part] = send(
                at(3, columns=part), at(5, columns=part), peer(2)
            )
            f["side_plus", part] = send(
                at(3, columns=part), at(6, columns=part), peer(1)
            )
    for (at, peer), f in zip(sides, flights):
        arrived([f["minus", high_rows], f["plus", low_rows]])
    for slot in (3, 1, 2):
        cross(slot)

    scale_t = LOG2E * TW**-0.5
    scale_s = LOG2E * SW**-0.5

    def dots(model, p, u0, count):
        rows = slice(u0 * UNIT, (u0 + count) * UNIT)
        lanes = slice(TW, W) if model else slice(0, TW)
        width = SW if model else TW
        logit, scale = ((lt, scale_t), (ls, scale_s))[model]
        logit[p, rows, :] = scale * dot_nt(
            img[u0 : u0 + count, :, lanes].reshape(count * UNIT, width),
            txt[2 * p : 2 * p + 2, :, lanes].reshape(2 * UNIT, width),
        )

    def fold(model, p, u):
        logit = (lt, ls)[model]
        rows = slice(u * UNIT, (u + 1) * UNIT)
        left, right = logit[p, rows, 0:128], logit[p, rows, 128:256]
        old = rm[model, rows, :]
        new = jnp.maximum(old, jnp.maximum(left, right))
        rm[model, rows, :] = new
        rs[model, rows, :] = (
            rs[model, rows, :] * jnp.exp2(old - new) + jnp.exp2(left - new) + jnp.exp2(right - new)
        )
        for h, part in ((0, left), (1, right)):
            lanes = slice(h * 128, h * 128 + 128)
            part = part.reshape(16, 8, 128)
            old = cm[model, p, :, lanes]
            new = jnp.maximum(old, jnp.max(part, axis=0))
            cm[model, p, :, lanes] = new
            cs[model, p, :, lanes] = cs[model, p, :, lanes] * jnp.exp2(old - new) + jnp.sum(
                jnp.exp2(part - new[None]), axis=0
            )

    def blocks(todo):
        for model, p, u0, count in todo:
            dots(model, p, u0, count)
            for u in range(u0, u0 + count):
                fold(model, p, u)

    def largest(ref, count):
        best = jnp.zeros((8, SW), F32)
        for n in range(count):
            part = jnp.abs(ref[n, :, TW:W].astype(F32)).reshape(16, 8, SW)
            best = jnp.maximum(best, jnp.max(part, axis=0))
        return jnp.broadcast_to(jnp.max(best, axis=(0, 1), keepdims=True), (1, 128))

    arrived(crossings)
    crossings.clear()
    blocks([(model, p, 0, 4) for p in range(4) for model in range(2)])
    for (at, peer), f in zip(sides, flights):
        arrived([f["far", low_rows], f["far", high_rows]])
        for part in (teacher_part, student_part):
            f["side_far", part] = send(at(4, columns=part), at(7, columns=part), peer(3))
    cross(4)
    arrived(crossings)
    crossings.clear()
    blocks([(model, 4, 0, 5) for model in range(2)])
    blocks([(model, p, 4, 1) for p in range(4) for model in range(2)])

    for model, part in enumerate((teacher_part, student_part)):
        for (at, peer), f in reversed(list(zip(sides, flights))):
            for slot, name in ((5, "side_minus"), (6, "side_plus"), (7, "side_far")):
                f[name, part].wait_recv()
                if at is text_at:
                    cross(slot, part)
        blocks([(model, p, 5, 3) for p in range(5)])
        arrived(crossings)
        crossings.clear()
        blocks([(model, p, u0, 4) for p in range(5, 8) for u0 in (0, 4)])

    image_top = jnp.maximum(largest(img, NI), TINY)
    text_top = jnp.maximum(largest(txt, 2 * NP), TINY)
    top[0] = jnp.broadcast_to(image_top, (8, 128))
    top_flight = send(top.at[0], top.at[1], t_peer(1, 0))
    for slot, (a, r) in enumerate(SLOTS):
        rows = slice(slot * UNIT, slot * UNIT + UNIT)
        for model in range(2):
            peaks = rm[model, rows, :].T
            totals = rs[model, rows, :].T
            peak = jnp.max(peaks, axis=0, keepdims=True)
            total = jnp.sum(totals * jnp.exp2(peaks - peak), axis=0, keepdims=True)
            lse = log_sum(peak, total)
            for flip in range(2):
                row = (a ^ flip) * 2 + model
                rmsg[flip, r, row : row + 1, :] = lse
            peaks = cm[model, slot]
            peak = jnp.max(peaks, axis=0, keepdims=True)
            total = jnp.sum(cs[model, slot] * jnp.exp2(peaks - peak), axis=0, keepdims=True)
            lse = log_sum(peak, total)
            for cc in range(2):
                for flip in range(4):
                    row = (((cc * 2 + a) ^ flip) * 2) + model
                    cmsg[flip, r, row : row + 1, :] = lse[:, cc * 128 : cc * 128 + 128]
    for flip in range(2):
        for r in range(4):
            rmsg[flip, r, 4:8, :] = jnp.broadcast_to(text_top, (4, 128))

    flying = [
        send(cmsg.at[cc * 2 + SLOTS[q][0]], crx.at[2 * BACK[q] + cc], t_peer(cc, q))
        for q in range(7, -1, -1)
        for cc in range(2)
        if q or cc
    ]
    flying += [
        send(rmsg.at[SLOTS[q][0]], rrx.at[BACK[q]], i_peer(q)) for q in range(7, 0, -1)
    ]
    for b in range(NI // 2):
        turned = img[2 * b : 2 * b + 2, :, TW:W].reshape(2 * UNIT, SW).T
        ist[:, b * 512 : b * 512 + 256] = turned
        ist[:, b * 512 + 256 : b * 512 + 512] = turned
    arrived(flying)

    def combine(own, parts):
        peak = own
        for part in parts:
            peak = jnp.maximum(peak, part)
        total = jnp.exp2(own - peak)
        for part in parts:
            total = total + jnp.exp2(part - peak)
        return log_sum(peak, total)

    for r in range(4):
        rlse[r] = combine(
            rmsg[0, r], [rrx[q, (r - SLOTS[q][1]) % 4] for q in range(1, 8)]
        )
        clse[r] = combine(
            cmsg[0, r], [crx[j, (r - SLOTS[j // 2][1]) % 4] for j in range(1, 16)]
        )
    gap = (rlse[0, 1:2, :] - rlse[0, 0:1, :]) + (clse[0, 1:2, :] - clse[0, 0:1, :])

    image_code = CODE * SW**-0.5 / text_top[0:1, 0:1]
    grad_flights = []

    def tiles(b, p, rows_lse, diverge):
        rows = slice(b * 256, b * 256 + 256)
        a, r = SLOTS[p]
        lse_t, lse_s = rows_lse
        for h in range(2):
            lanes = slice(h * 128, h * 128 + 128)
            row = (h * 2 + a) * 2
            t = lt[p, rows, lanes]
            s = ls[p, rows, lanes]
            teacher = jnp.exp2(t - lse_t) + jnp.exp2(t - clse[r, row : row + 1, :])
            student = jnp.exp2(s - lse_s) + jnp.exp2(s - clse[r, row + 1 : row + 2, :])
            diverge = diverge + jnp.sum((teacher * (t - s)).reshape(32, 8, 128), axis=0)
            delta = student - teacher
            high = delta.astype(BF16)
            low = (delta - high.astype(F32)).astype(BF16)
            d[p, b, 0:256, lanes] = high
            d[p, b, 256:512, lanes] = low
        return diverge

    def turned_lse(b):
        found = []
        for model in range(2):
            columns = []
            for slot in (2 * b, 2 * b + 1):
                a, r = SLOTS[slot]
                row = 2 * a + model
                columns.append(jnp.broadcast_to(rlse[r, row : row + 1, :], (128, 128)).T)
            found.append(jnp.concatenate(columns, axis=0))
        return found

    diverge = jnp.zeros((8, 128), F32)
    rows_lse = turned_lse(3)
    for p in range(NP):
        diverge = tiles(3, p, rows_lse, diverge)
    for b in (3, 2, 1, 0):
        total = jnp.zeros((512, SW), F32)
        rows_lse = turned_lse(b - 1) if b else None
        for p in range(NP):
            if b:
                diverge = tiles(b - 1, p, rows_lse, diverge)
            weights = txt[2 * p : 2 * p + 2, :, TW:W].reshape(2 * UNIT, SW)
            total = total + jnp.dot(d[p, b], weights, preferred_element_type=F32)
        total = total[0:256] + total[256:512]
        for h in (1, 0):
            slot = 2 * b + h
            part = total[h * 128 : h * 128 + 128]
            if slot == 0:
                out[0:UNIT] = part
            else:
                isend[slot] = encode(part * image_code)
                grad_flights.append(send(isend.at[slot], irecv.at[BACK[slot]], i_peer(slot)))

    first_row = lax.broadcasted_iota(jnp.int32, (8, 128), 0) == 0
    lsend[0, 0:8] = diverge + jnp.where(first_row, jnp.broadcast_to(gap, (8, 128)), 0.0)
    loss_flights = [
        send(lsend.at[0, 0:8], lrx_i.at[BACK[q]], i_peer(q)) for q in range(7, 0, -1)
    ]
    top_flight.wait_recv()
    chip_top = jnp.maximum(image_top, top[1, 0:1, :])
    text_code = CODE * SW**-0.5 / chip_top[0:1, 0:1]

    crossed = {}

    def pass_on(slot):
        crossed[slot].wait_recv()
        part = keep[slot] + xrecv[slot]
        if slot == 0:
            keep[0] = part
        else:
            tsend[slot] = encode(part * text_code)
            grad_flights.append(send(tsend.at[slot], trecv.at[BACK[slot]], t_peer(0, slot)))

    for p in range(NP - 1, -1, -1):
        part = jnp.dot(ist[...], d[p].reshape(2048, 256), preferred_element_type=F32)
        keep[p] = part[:, 0:128]
        xsend[p] = part[:, 128:256]
        crossed[p] = send(xsend.at[p], xrecv.at[p], t_peer(1, 0))
        if p < NP - 1:
            pass_on(p + 1)
        if p == 3:
            arrived(loss_flights)
            loss_part = lsend[0, 0:8]
            for q in range(1, 8):
                loss_part = loss_part + lrx_i[q]
            lsend[1, 0:8] = loss_part
            lsend[1, 8:16] = jnp.broadcast_to(chip_top, (8, 128))
            loss_flights = [
                send(lsend.at[1], lrx_t.at[2 * BACK[j // 2] + j % 2], t_peer(j % 2, j // 2))
                for j in range(15, 0, -1)
            ]
    pass_on(0)

    arrived(loss_flights)
    loss_part = lsend[1, 0:8]
    for q in range(1, 16):
        loss_part = loss_part + lrx_t[q, 0:8]
    loss = jnp.sum(loss_part, axis=(0, 1), keepdims=True) * (LN2 / (2.0 * pairs))
    out[2 * UNIT : 2 * UNIT + 8] = jnp.broadcast_to(loss, (8, SW))

    arrived(grad_flights)
    image_total = out[0:UNIT] * SW**-0.5
    text_total = keep[0] * SW**-0.5
    for q in range(1, 8):
        image_total = image_total + decode(irecv[q]) * (rrx[q, 0, 4:5, 0:1] * (1.0 / CODE))
        text_total = text_total + decode(trecv[q]) * (lrx_t[2 * q, 8:9, 0:1] * (1.0 / CODE))
    out[0:UNIT] = image_total
    out[UNIT : 2 * UNIT] = text_total.T
    for copy in begun:
        copy.wait_send()


def local(teacher_image, teacher_text, student_image, student_text):
    pairs = teacher_image.shape[0] * lax.axis_size("img") * lax.axis_size("txt")
    vmem = pltpu.VMEM
    result = pl.pallas_call(
        functools.partial(kernel, pairs),
        out_shape=jax.ShapeDtypeStruct((2 * UNIT + 8, SW), F32),
        in_specs=[pl.BlockSpec(memory_space=pl.ANY)] * 4,
        out_specs=pl.BlockSpec(memory_space=vmem),
        scratch_shapes=[
            vmem((NI, UNIT, W), BF16),
            vmem((2 * NP, UNIT, W), BF16),
            vmem((NP, NI * UNIT, 256), F32),
            vmem((NP, NI * UNIT, 256), F32),
            vmem((2, NI * UNIT, 128), F32),
            vmem((2, NI * UNIT, 128), F32),
            vmem((2, NP, 8, 256), F32),
            vmem((2, NP, 8, 256), F32),
            vmem((NP, NI // 2, 512, 256), BF16),
            vmem((SW, 2 * NI * UNIT), BF16),
            vmem((2, 4, 8, 128), F32),
            vmem((4, 4, 8, 128), F32),
            vmem((8, 4, 8, 128), F32),
            vmem((16, 4, 8, 128), F32),
            vmem((4, 8, 128), F32),
            vmem((4, 8, 128), F32),
            vmem((8, UNIT, SW), BF16),
            vmem((8, UNIT, SW), BF16),
            vmem((8, SW, UNIT), F32),
            vmem((8, SW, UNIT), F32),
            vmem((8, SW, UNIT), F32),
            vmem((8, SW, UNIT), BF16),
            vmem((8, SW, UNIT), BF16),
            vmem((2, 16, 128), F32),
            vmem((8, 8, 128), F32),
            vmem((16, 16, 128), F32),
            vmem((2, 8, 128), F32),
            pltpu.SemaphoreType.DMA((4,)),
            pltpu.SemaphoreType.DMA((128,)),
            pltpu.SemaphoreType.DMA((128,)),
        ],
        compiler_params=pltpu.CompilerParams(
            collective_id=0, has_side_effects=True, vmem_limit_bytes=62 * 2**20
        ),
        cost_estimate=pl.CostEstimate(
            flops=16_000_000_000, bytes_accessed=1_500_000, transcendentals=20_000_000
        ),
    )(teacher_image, teacher_text, student_image, student_text)
    return result[2 * UNIT, 0], result[0:UNIT], result[UNIT : 2 * UNIT]


def solution(mesh):
    in_specs = (
        P(("img", "txt"), None),
        P(("txt", "img"), None),
        P(("img", "txt"), None),
        P(("txt", "img"), None),
    )
    out_specs = (P(), P(("img", "txt"), None), P(("txt", "img"), None))
    return jax.shard_map(local, mesh=mesh, in_specs=in_specs, out_specs=out_specs, check_vma=False)
```

time: 111 us -> 88.6 us (0.80)
  Pallas kernels: 106 us -> 84.8 us
    pallas_call x1, Pallas kernels: 106 us -> 84.8 us  [local(): pl.pallas_call(functools.partial(kernel, pairs), out_shape=jax.ShapeDtype...]
    unnamed x4 -> x0, local copies, waits for them, and re-layouts: 2.42 us -> none
    slice x1 -> x2, local copies, waits for them, and re-layouts: 1.19 us -> 3.04 us  [local(): return (result[2 * UNIT, 0], result[0:UNIT], result[UNIT:2 * UNIT])]
where the time goes in v2:
time: 88.6 us; the launch traced here: 88.5 us
  Pallas kernels  84.8 us (96%)
  local copies, waits for them, and re-layouts  3.04 us (3%)
    pallas_call x1, Pallas kernels, local(): pl.pallas_call(functools.partial(kernel, pairs), out_shape=jax.ShapeDtype...  84.8 us
    slice x2, local copies, waits for them, and re-layouts, local(): return (result[2 * UNIT, 0], result[0:UNIT], result[UNIT:2 * UNIT])  3.04 us

profile of v2, /device:TPU:1, one launch (start us, length us, event | category | flops | bytes accessed | tf_op | source)
XLA Modules:
  0.0 88.5 jit_solution(7399053467264856846)
XLA Ops:
  0.6 84.8 %shard_map.67 = f32[264,512]{1,0:T(8,128)} custom-call(bf16[128,1280]{1,0:T(8,128)(2,1)} %ti.1, bf16[128,1280]{1,0:T(8,128)(2,1)} %tt.1, bf16[128,512]{1,0:T(8,128)(2,1)} %si.1, bf16[128,512]{1,0:T(8,128)(2,1)} %st.1), custom_call_target="tpu_custom_call" | custom-call | flops 16000000000 | bytes 1500000 | tf_op jit(solution)/shard_map/pallas_call | solution.py:402
  85.4 1.9 %fusion = (f32[128,512]{1,0:T(8,128)}, f32[128,512]{1,0:T(8,128)}) fusion(f32[264,512]{1,0:T(8,128)} %shard_map.67), kind=kLoop, calls=%fused_computation | loop fusion | bytes 1048576 | tf_op jit(solution)/shard_map/slice | solution.py:446
  87.3 1.2 %slice.9 = f32[1,1]{1,0:T(1,128)} slice(f32[264,512]{1,0:T(8,128)} %shard_map.67), slice={[256:257], [0:1]} | slice | bytes 8 | tf_op jit(solution)/shard_map/slice | solution.py:446

commit v3 on v2

--- a/solution.py
+++ b/solution.py
@@ -104,6 +104,7 @@
     rs[...] = jnp.zeros(rs.shape, F32)
     cm[...] = jnp.full(cm.shape, LOW, F32)
     cs[...] = jnp.zeros(cs.shape, F32)
+    rmsg[...] = jnp.zeros(rmsg.shape, F32)
     pl.semaphore_wait(barrier, 7)
     for copy in loads:
         copy.wait()
@@ -115,6 +116,9 @@
         return txt.at[2 * slot, rows[0] : rows[1], columns[0] : columns[1]]
 
     low_rows, high_rows = (0, 64), (64, 128)
+    third_rows, last_rows, second_rows, first_rows = (64, 96), (96, 128), (32, 64), (0, 32)
+    minus_relief, plus_relief = (0, 16), (112, 128)
+    minus_rest, plus_rest = (16, 128), (0, 112)
     teacher_part, student_part = (0, TW), (TW, W)
     sides = ((image_at, i_peer), (text_at, functools.partial(t_peer, 0)))
     crossings = []
@@ -126,31 +130,48 @@
         )
 
     flights = [{} for _ in sides]
-    for first, second in ((low_rows, high_rows), (high_rows, low_rows)):
-        for (at, peer), f in zip(sides, flights):
-            f["minus", first] = send(at(0, first), at(1, first), peer(2))
-            f["plus", second] = send(at(0, second), at(2, second), peer(1))
-            f["side", first] = send(at(0, first), at(3, first), peer(3))
+    for (at, peer), f in zip(sides, flights):
+        f["minus", 0] = send(at(0, low_rows), at(1, low_rows), peer(2))
+        f["plus", 0] = send(at(0, high_rows), at(2, high_rows), peer(1))
+        f["side", 0] = send(at(0, low_rows), at(3, low_rows), peer(3))
+    for (at, peer), f in zip(sides, flights):
+        f["minus", 1] = send(at(0, third_rows), at(1, third_rows), peer(2))
+        f["plus", 1] = send(at(0, second_rows), at(2, second_rows), peer(1))
+        f["side", 1] = send(at(0, high_rows), at(3, high_rows), peer(3))
     cross(0)
     for (at, peer), f in zip(sides, flights):
-        f["minus", low_rows].wait_recv()
-        f["far", low_rows] = send(at(1, low_rows), at(4, low_rows), peer(2))
-    for (at, peer), f in zip(sides, flights):
-        f["plus", high_rows].wait_recv()
-        f["far", high_rows] = send(at(2, high_rows), at(4, high_rows), peer(1))
-    for (at, peer), f in zip(sides, flights):
-        arrived([f["side", low_rows], f["side", high_rows]])
+        f["minus", 0].wait_recv()
+        f["far", 0] = send(at(1, low_rows), at(4, low_rows), peer(2))
+        f["relief", 0] = send(at(1, minus_relief), at(5, minus_relief), peer(3))
+        f["minus", 2] = send(at(0, last_rows), at(1, last_rows), peer(2))
+    for (at, peer), f in zip(sides, flights):
+        f["plus", 0].wait_recv()
+        f["far", 1] = send(at(2, high_rows), at(4, high_rows), peer(1))
+        f["relief", 1] = send(at(2, plus_relief), at(6, plus_relief), peer(3))
+        f["plus", 2] = send(at(0, first_rows), at(2, first_rows), peer(1))
+    for (at, peer), f in zip(sides, flights):
+        arrived([f["side", 0], f["side", 1]])
         for part in (teacher_part, student_part):
-            f["side_minus", part] = send(
-                at(3, columns=part), at(5, columns=part), peer(2)
+            f["side_minus", part] = send(at(3, minus_rest, part), at(5, minus_rest, part), peer(2))
+            f["side_plus", part] = send(at(3, plus_rest, part), at(6, plus_rest, part), peer(1))
+    cross(3)
+    for (at, peer), f in zip(sides, flights):
+        for n, rows in enumerate((low_rows, high_rows)):
+            f["far", n].wait_recv()
+            f["side_far", n, teacher_part] = send(
+                at(4, rows, teacher_part), at(7, rows, teacher_part), peer(3)
             )
-            f["side_plus", part] = send(
-                at(3, columns=part), at(6, columns=part), peer(1)
+    for (at, peer), f in zip(sides, flights):
+        for n, rows in enumerate((low_rows, high_rows)):
+            f["side_far", n, student_part] = send(
+                at(4, rows, student_part), at(7, rows, student_part), peer(3)
             )
-    for (at, peer), f in zip(sides, flights):
-        arrived([f["minus", high_rows], f["plus", low_rows]])
-    for slot in (3, 1, 2):
-        cross(slot)
+    cross(4)
+    for (at, peer), f in reversed(list(zip(sides, flights))):
+        arrived([f["minus", 1], f["plus", 1], f["minus", 2], f["plus", 2]])
+        if at is text_at:
+            cross(1)
+            cross(2)
 
     scale_t = LOG2E * TW**-0.5
     scale_s = LOG2E * SW**-0.5
@@ -200,21 +221,16 @@
 
     arrived(crossings)
     crossings.clear()
-    blocks([(model, p, 0, 4) for p in range(4) for model in range(2)])
-    for (at, peer), f in zip(sides, flights):
-        arrived([f["far", low_rows], f["far", high_rows]])
-        for part in (teacher_part, student_part):
-            f["side_far", part] = send(at(4, columns=part), at(7, columns=part), peer(3))
-    cross(4)
-    arrived(crossings)
-    crossings.clear()
-    blocks([(model, 4, 0, 5) for model in range(2)])
-    blocks([(model, p, 4, 1) for p in range(4) for model in range(2)])
+    blocks([(model, p, 0, 5) for p in range(5) for model in range(2)])
 
     for model, part in enumerate((teacher_part, student_part)):
         for (at, peer), f in reversed(list(zip(sides, flights))):
-            for slot, name in ((5, "side_minus"), (6, "side_plus"), (7, "side_far")):
-                f[name, part].wait_recv()
+            for slot, names in (
+                (5, (("relief", 0), ("side_minus", part))),
+                (6, (("relief", 1), ("side_plus", part))),
+                (7, (("side_far", 0, part), ("side_far", 1, part))),
+            ):
+                arrived([f[name] for name in names if model == 0 or name[0] != "relief"])
                 if at is text_at:
                     cross(slot, part)
         blocks([(model, p, 5, 3) for p in range(5)])
@@ -222,10 +238,6 @@
         crossings.clear()
         blocks([(model, p, u0, 4) for p in range(5, 8) for u0 in (0, 4)])
 
-    image_top = jnp.maximum(largest(img, NI), TINY)
-    text_top = jnp.maximum(largest(txt, 2 * NP), TINY)
-    top[0] = jnp.broadcast_to(image_top, (8, 128))
-    top_flight = send(top.at[0], top.at[1], t_peer(1, 0))
     for slot, (a, r) in enumerate(SLOTS):
         rows = slice(slot * UNIT, slot * UNIT + UNIT)
         for model in range(2):
@@ -245,9 +257,6 @@
                 for flip in range(4):
                     row = (((cc * 2 + a) ^ flip) * 2) + model
                     cmsg[flip, r, row : row + 1, :] = lse[:, cc * 128 : cc * 128 + 128]
-    for flip in range(2):
-        for r in range(4):
-            rmsg[flip, r, 4:8, :] = jnp.broadcast_to(text_top, (4, 128))
 
     flying = [
         send(cmsg.at[cc * 2 + SLOTS[q][0]], crx.at[2 * BACK[q] + cc], t_peer(cc, q))
@@ -258,6 +267,10 @@
     flying += [
         send(rmsg.at[SLOTS[q][0]], rrx.at[BACK[q]], i_peer(q)) for q in range(7, 0, -1)
     ]
+    image_top = jnp.maximum(largest(img, NI), TINY)
+    text_top = jnp.maximum(largest(txt, 2 * NP), TINY)
+    top[0] = jnp.broadcast_to(image_top, (8, 128))
+    top_flight = send(top.at[0], top.at[1], t_peer(1, 0))
     for b in range(NI // 2):
         turned = img[2 * b : 2 * b + 2, :, TW:W].reshape(2 * UNIT, SW).T
         ist[:, b * 512 : b * 512 + 256] = turned
@@ -283,7 +296,7 @@
     gap = (rlse[0, 1:2, :] - rlse[0, 0:1, :]) + (clse[0, 1:2, :] - clse[0, 0:1, :])
 
     image_code = CODE * SW**-0.5 / text_top[0:1, 0:1]
-    grad_flights = []
+    image_flights, text_flights = [], []
 
     def tiles(b, p, rows_lse, diverge):
         rows = slice(b * 256, b * 256 + 256)
@@ -315,18 +328,21 @@
             found.append(jnp.concatenate(columns, axis=0))
         return found
 
-    diverge = jnp.zeros((8, 128), F32)
-    rows_lse = turned_lse(3)
-    for p in range(NP):
-        diverge = tiles(3, p, rows_lse, diverge)
-    for b in (3, 2, 1, 0):
-        total = jnp.zeros((512, SW), F32)
-        rows_lse = turned_lse(b - 1) if b else None
-        for p in range(NP):
-            if b:
-                diverge = tiles(b - 1, p, rows_lse, diverge)
-            weights = txt[2 * p : 2 * p + 2, :, TW:W].reshape(2 * UNIT, SW)
-            total = total + jnp.dot(d[p, b], weights, preferred_element_type=F32)
+    FAR, NEAR = (7, 6, 5, 4), (3, 2, 1, 0)
+    row_lse = {}
+
+    def delta_tiles(b, pairs_of_text, diverge):
+        if b not in row_lse:
+            row_lse[b] = turned_lse(b)
+        for p in pairs_of_text:
+            diverge = tiles(b, p, row_lse[b], diverge)
+        return diverge
+
+    def image_dot(total, b, p):
+        weights = txt[2 * p : 2 * p + 2, :, TW:W].reshape(2 * UNIT, SW)
+        return total + jnp.dot(d[p, b], weights, preferred_element_type=F32)
+
+    def image_send(total, b):
         total = total[0:256] + total[256:512]
         for h in (1, 0):
             slot = 2 * b + h
@@ -335,62 +351,105 @@
                 out[0:UNIT] = part
             else:
                 isend[slot] = encode(part * image_code)
-                grad_flights.append(send(isend.at[slot], irecv.at[BACK[slot]], i_peer(slot)))
-
-    first_row = lax.broadcasted_iota(jnp.int32, (8, 128), 0) == 0
-    lsend[0, 0:8] = diverge + jnp.where(first_row, jnp.broadcast_to(gap, (8, 128)), 0.0)
-    loss_flights = [
-        send(lsend.at[0, 0:8], lrx_i.at[BACK[q]], i_peer(q)) for q in range(7, 0, -1)
-    ]
-    top_flight.wait_recv()
-    chip_top = jnp.maximum(image_top, top[1, 0:1, :])
-    text_code = CODE * SW**-0.5 / chip_top[0:1, 0:1]
+                image_flights.append(send(isend.at[slot], irecv.at[BACK[slot]], i_peer(slot)))
 
     crossed = {}
 
-    def pass_on(slot):
+    def text_part(p):
+        part = jnp.dot(ist[...], d[p].reshape(2048, 256), preferred_element_type=F32)
+        keep[p] = part[:, 0:128]
+        xsend[p] = part[:, 128:256]
+
+    def text_cross(p):
+        crossed[p] = send(xsend.at[p], xrecv.at[p], t_peer(1, 0))
+
+    def text_send(slot):
         crossed[slot].wait_recv()
         part = keep[slot] + xrecv[slot]
         if slot == 0:
             keep[0] = part
         else:
             tsend[slot] = encode(part * text_code)
-            grad_flights.append(send(tsend.at[slot], trecv.at[BACK[slot]], t_peer(0, slot)))
-
-    for p in range(NP - 1, -1, -1):
-        part = jnp.dot(ist[...], d[p].reshape(2048, 256), preferred_element_type=F32)
-        keep[p] = part[:, 0:128]
-        xsend[p] = part[:, 128:256]
-        crossed[p] = send(xsend.at[p], xrecv.at[p], t_peer(1, 0))
-        if p < NP - 1:
-            pass_on(p + 1)
-        if p == 3:
-            arrived(loss_flights)
-            loss_part = lsend[0, 0:8]
-            for q in range(1, 8):
-                loss_part = loss_part + lrx_i[q]
-            lsend[1, 0:8] = loss_part
-            lsend[1, 8:16] = jnp.broadcast_to(chip_top, (8, 128))
-            loss_flights = [
-                send(lsend.at[1], lrx_t.at[2 * BACK[j // 2] + j % 2], t_peer(j % 2, j // 2))
-                for j in range(15, 0, -1)
-            ]
-    pass_on(0)
-
+            text_flights.append(send(tsend.at[slot], trecv.at[BACK[slot]], t_peer(0, slot)))
+
+    diverge = jnp.zeros((8, 128), F32)
+    diverge = delta_tiles(3, FAR + NEAR, diverge)
+    total = jnp.zeros((512, SW), F32)
+    for n, p in enumerate(FAR + NEAR):
+        diverge = delta_tiles(2, (p,), diverge)
+        total = image_dot(total, 3, p)
+    image_send(total, 3)
+    total = jnp.zeros((512, SW), F32)
+    for n, p in enumerate(FAR + NEAR):
+        if n < 4:
+            diverge = delta_tiles(1, (p,), diverge)
+            diverge = delta_tiles(0, (p,), diverge)
+        total = image_dot(total, 2, p)
+    image_send(total, 2)
+    top_flight.wait_recv()
+    chip_top = jnp.maximum(image_top, top[1, 0:1, :])
+    text_code = CODE * SW**-0.5 / chip_top[0:1, 0:1]
+    for some, others in ((FAR[:2], NEAR[:2]), (FAR[2:], NEAR[2:])):
+        for p in others:
+            diverge = delta_tiles(1, (p,), diverge)
+            diverge = delta_tiles(0, (p,), diverge)
+        for p in some:
+            text_part(p)
+        for p in some:
+            text_cross(p)
+    text_send(7)
+    text_send(6)
+    first_row = lax.broadcasted_iota(jnp.int32, (8, 128), 0) == 0
+    lsend[0, 0:8] = diverge + jnp.where(first_row, jnp.broadcast_to(gap, (8, 128)), 0.0)
+    lsend[0, 8:16] = jnp.broadcast_to(text_top, (8, 128))
+    loss_flights = [send(lsend.at[0], lrx_i.at[BACK[q]], i_peer(q)) for q in range(7, 0, -1)]
+    total = jnp.zeros((512, SW), F32)
+    for p in FAR + NEAR:
+        total = image_dot(total, 1, p)
+    image_send(total, 1)
+    text_send(5)
+    text_send(4)
+    total = jnp.zeros((512, SW), F32)
+    for p in FAR + NEAR:
+        total = image_dot(total, 0, p)
+    text_part(3)
+    text_part(2)
+    image_send(total, 0)
+    text_cross(3)
+    text_cross(2)
+    text_part(1)
+    text_part(0)
+    text_cross(1)
+    text_cross(0)
+    for slot in NEAR:
+        text_send(slot)
+
+    arrived(loss_flights)
+    loss_part = lsend[0, 0:8]
+    for q in range(1, 8):
+        loss_part = loss_part + lrx_i[q, 0:8]
+    lsend[1, 0:8] = loss_part
+    lsend[1, 8:16] = jnp.broadcast_to(chip_top, (8, 128))
+    loss_flights = [
+        send(lsend.at[1], lrx_t.at[2 * BACK[j // 2] + j % 2], t_peer(j % 2, j // 2))
+        for j in range(15, 0, -1)
+    ]
+
+    image_total = out[0:UNIT] * SW**-0.5
+    for q, flight in zip([BACK[q] for q in (7, 6, 5, 4, 3, 2, 1)], image_flights):
+        flight.wait_recv()
+        image_total = image_total + decode(irecv[q]) * (lrx_i[q, 8:9, 0:1] * (1.0 / CODE))
+    out[0:UNIT] = image_total
     arrived(loss_flights)
     loss_part = lsend[1, 0:8]
     for q in range(1, 16):
         loss_part = loss_part + lrx_t[q, 0:8]
     loss = jnp.sum(loss_part, axis=(0, 1), keepdims=True) * (LN2 / (2.0 * pairs))
     out[2 * UNIT : 2 * UNIT + 8] = jnp.broadcast_to(loss, (8, SW))
-
-    arrived(grad_flights)
-    image_total = out[0:UNIT] * SW**-0.5
     text_total = keep[0] * SW**-0.5
-    for q in range(1, 8):
-        image_total = image_total + decode(irecv[q]) * (rrx[q, 0, 4:5, 0:1] * (1.0 / CODE))
+    for q, flight in zip([BACK[q] for q in (7, 6, 5, 4, 3, 2, 1)], text_flights):
+        flight.wait_recv()
         text_total = text_total + decode(trecv[q]) * (lrx_t[2 * q, 8:9, 0:1] * (1.0 / CODE))
-    out[0:UNIT] = image_total
     out[UNIT : 2 * UNIT] = text_total.T
     for copy in begun:
         copy.wait_send()
@@ -429,7 +488,7 @@
             vmem((8, SW, UNIT), BF16),
             vmem((8, SW, UNIT), BF16),
             vmem((2, 16, 128), F32),
-            vmem((8, 8, 128), F32),
+            vmem((8, 16, 128), F32),
             vmem((16, 16, 128), F32),
             vmem((2, 8, 128), F32),
             pltpu.SemaphoreType.DMA((4,)),

time: 88.6 us -> 82.8 us (0.935)
  Pallas kernels: 84.8 us -> 79 us
    pallas_call x1, Pallas kernels: 84.8 us -> 79 us  [local(): pl.pallas_call(functools.partial(kernel, pairs), out_shape=jax.ShapeDtype...]
where the time goes in v3:
time: 82.8 us; the launch traced here: 82.6 us
  Pallas kernels  79 us (95%)
  local copies, waits for them, and re-layouts  3.04 us (4%)
    pallas_call x1, Pallas kernels, local(): pl.pallas_call(functools.partial(kernel, pairs), out_shape=jax.ShapeDtype...  79 us
    slice x2, local copies, waits for them, and re-layouts, local(): return (result[2 * UNIT, 0], result[0:UNIT], result[UNIT:2 * UNIT])  3.04 us

profile of v3, /device:TPU:1, one launch (start us, length us, event | category | flops | bytes accessed | tf_op | source)
XLA Modules:
  0.0 82.6 jit_solution(10686757926260426589)
XLA Ops:
  0.6 79.0 %shard_map.67 = f32[264,512]{1,0:T(8,128)} custom-call(bf16[128,1280]{1,0:T(8,128)(2,1)} %ti.1, bf16[128,1280]{1,0:T(8,128)(2,1)} %tt.1, bf16[128,512]{1,0:T(8,128)(2,1)} %si.1, bf16[128,512]{1,0:T(8,128)(2,1)} %st.1), custom_call_target="tpu_custom_call" | custom-call | flops 16000000000 | bytes 1500000 | tf_op jit(solution)/shard_map/pallas_call | solution.py:461
  79.6 1.9 %fusion = (f32[128,512]{1,0:T(8,128)}, f32[128,512]{1,0:T(8,128)}) fusion(f32[264,512]{1,0:T(8,128)} %shard_map.67), kind=kLoop, calls=%fused_computation | loop fusion | bytes 1048576 | tf_op jit(solution)/shard_map/slice | solution.py:505
  81.4 1.2 %slice.9 = f32[1,1]{1,0:T(1,128)} slice(f32[264,512]{1,0:T(8,128)} %shard_map.67), slice={[256:257], [0:1]} | slice | bytes 8 | tf_op jit(solution)/shard_map/slice | solution.py:505

commit v4 on v3

--- a/solution.py
+++ b/solution.py
@@ -239,6 +239,23 @@
         blocks([(model, p, u0, 4) for p in range(5, 8) for u0 in (0, 4)])
 
     for slot, (a, r) in enumerate(SLOTS):
+        for model in range(2):
+            peaks = cm[model, slot]
+            peak = jnp.max(peaks, axis=0, keepdims=True)
+            total = jnp.sum(cs[model, slot] * jnp.exp2(peaks - peak), axis=0, keepdims=True)
+            lse = log_sum(peak, total)
+            for cc in range(2):
+                for flip in range(4):
+                    row = (((cc * 2 + a) ^ flip) * 2) + model
+                    cmsg[flip, r, row : row + 1, :] = lse[:, cc * 128 : cc * 128 + 128]
+
+    flying = [
+        send(cmsg.at[cc * 2 + SLOTS[q][0]], crx.at[2 * BACK[q] + cc], t_peer(cc, q))
+        for q in range(7, -1, -1)
+        for cc in range(2)
+        if q or cc
+    ]
+    for slot, (a, r) in enumerate(SLOTS):
         rows = slice(slot * UNIT, slot * UNIT + UNIT)
         for model in range(2):
             peaks = rm[model, rows, :].T
@@ -249,21 +266,6 @@
             for flip in range(2):
                 row = (a ^ flip) * 2 + model
                 rmsg[flip, r, row : row + 1, :] = lse
-            peaks = cm[model, slot]
-            peak = jnp.max(peaks, axis=0, keepdims=True)
-            total = jnp.sum(cs[model, slot] * jnp.exp2(peaks - peak), axis=0, keepdims=True)
-            lse = log_sum(peak, total)
-            for cc in range(2):
-                for flip in range(4):
-                    row = (((cc * 2 + a) ^ flip) * 2) + model
-                    cmsg[flip, r, row : row + 1, :] = lse[:, cc * 128 : cc * 128 + 128]
-
-    flying = [
-        send(cmsg.at[cc * 2 + SLOTS[q][0]], crx.at[2 * BACK[q] + cc], t_peer(cc, q))
-        for q in range(7, -1, -1)
-        for cc in range(2)
-        if q or cc
-    ]
     flying += [
         send(rmsg.at[SLOTS[q][0]], rrx.at[BACK[q]], i_peer(q)) for q in range(7, 0, -1)
     ]

time: 82.8 us -> 82.3 us (level)
  no operation moved by 1% of the time
where the time goes in v4:
time: 82.3 us; the launch traced here: 82.2 us
  Pallas kernels  78.5 us (95%)
  local copies, waits for them, and re-layouts  3.04 us (4%)
    pallas_call x1, Pallas kernels, local(): pl.pallas_call(functools.partial(kernel, pairs), out_shape=jax.ShapeDtype...  78.5 us
    slice x2, local copies, waits for them, and re-layouts, local(): return (result[2 * UNIT, 0], result[0:UNIT], result[UNIT:2 * UNIT])  3.04 us

profile of v4, /device:TPU:1, one launch (start us, length us, event | category | flops | bytes accessed | tf_op | source)
XLA Modules:
  0.0 82.2 jit_solution(17596615102253460446)
XLA Ops:
  0.6 78.5 %shard_map.67 = f32[264,512]{1,0:T(8,128)} custom-call(bf16[128,1280]{1,0:T(8,128)(2,1)} %ti.1, bf16[128,1280]{1,0:T(8,128)(2,1)} %tt.1, bf16[128,512]{1,0:T(8,128)(2,1)} %si.1, bf16[128,512]{1,0:T(8,128)(2,1)} %st.1), custom_call_target="tpu_custom_call" | custom-call | flops 16000000000 | bytes 1500000 | tf_op jit(solution)/shard_map/pallas_call | solution.py:463
  79.1 1.9 %fusion = (f32[128,512]{1,0:T(8,128)}, f32[128,512]{1,0:T(8,128)}) fusion(f32[264,512]{1,0:T(8,128)} %shard_map.67), kind=kLoop, calls=%fused_computation | loop fusion | bytes 1048576 | tf_op jit(solution)/shard_map/slice | solution.py:507
  81.0 1.2 %slice.9 = f32[1,1]{1,0:T(1,128)} slice(f32[264,512]{1,0:T(8,128)} %shard_map.67), slice={[256:257], [0:1]} | slice | bytes 8 | tf_op jit(solution)/shard_map/slice | solution.py:507
